TPU v7x, 32 devices: a whole 2x2x4 slice. The times are simulated.
32 devices in a mesh: depth: 4 (over x, core), tile: 8 (over z, y).
Axes of the slice: x: 2, y: 2, z: 4, core: 2. Of those that a mesh axis runs over, the one named last changes fastest.
Arguments:
- old_fields: float32 [2, 32, 512, 128], P(None, 'depth', 'tile'), may hold values from -6 to 6
- recv_block: int32 [4, 128], P('depth', 'tile'), may hold values from 0 to 511
- recv_count: int32 [4, 64], P('depth', 'tile'), may hold values from 0 to 2, as said below
- new_block: int32 [4, 128], P('depth', 'tile'), may hold values from 0 to 127
- moments: bfloat16 [4, 128, 4, 128, 128], P('depth', 'tile'), may hold values from -0.0606 to 0.0606, as said below
- new_volume: float32 [4, 1024, 128], P('depth', 'tile'), may hold values from 0.5 to 2
Outputs:
- new_fields: float32 [4, 1024, 2, 128], P('depth', 'tile')
Inputs may be any that keep to these rules, and one draw needn't show every extreme that they name: `recv_count`: the tiles of some quarter of each depth group hold 2 live slots from every source tile. `moments`: component 0 (intersection volumes) is nonnegative.
All inputs are finite; a program needn't handle non-finite values.
Results may differ from a plain program's by a relative error of at most 0.003.
Values may be sent and summed in bfloat16 or wider, within the bound.
A program may use at most 128 MiB of HBM per device.

v0:
```python
import jax
import jax.numpy as jnp
from jax import lax
from jax.sharding import PartitionSpec as P

CAP = 2


def with_halo(array, sides, width):
    for axis, dim in sides:
        size, length = (lax.axis_size(axis), array.shape[dim])
        up = [(i, (i + 1) % size) for i in range(size - 1)]
        down = [(j, i) for i, j in up]
        last = lax.slice_in_dim(array, length - width, length, axis=dim)
        initial = lax.slice_in_dim(array, 0, width, axis=dim)
        before = lax.ppermute(last, axis, up)
        after = lax.ppermute(initial, axis, down)
        array = jnp.concatenate([before, array, after], axis=dim)
    return array


def minmod(left_value, right_value):
    return (
        0.5
        * (jnp.sign(left_value) + jnp.sign(right_value))
        * jnp.minimum(jnp.abs(left_value), jnp.abs(right_value))
    )


def limited(centre, upper_side, lower_side):
    central = 0.5 * (upper_side - lower_side)
    return minmod(central, minmod(2.0 * (centre - lower_side), 2.0 * (upper_side - centre)))


def interior(offset, length, total):
    position = offset + jnp.arange(length, dtype=jnp.int32)
    return ((position > 0) & (position < total - 1)).astype(jnp.float32)


def per_device(old_fields, recv_block, recv_count, new_block, moments, new_volume):
    padded = with_halo(old_fields, (("depth", 1), ("tile", 2)), 1)
    centre = padded[:, 1:-1, 1:-1, :]
    layers = centre.shape[1]
    lateral = centre.shape[2]
    width_x = centre.shape[3]
    depth_keep = interior(lax.axis_index("depth") * layers, layers, layers * lax.axis_size("depth"))
    lateral_keep = interior(
        lax.axis_index("tile") * lateral, lateral, lateral * lax.axis_size("tile")
    )
    x_keep = interior(0, width_x, width_x)
    slope_depth = (
        limited(centre, padded[:, 2:, 1:-1, :], padded[:, :-2, 1:-1, :])
        * depth_keep[None, :, None, None]
    )
    slope_lateral = (
        limited(centre, padded[:, 1:-1, 2:, :], padded[:, 1:-1, :-2, :])
        * lateral_keep[None, None, :, None]
    )
    x_padded = jnp.pad(centre, ((0, 0), (0, 0), (0, 0), (1, 1)))
    slope_x = limited(centre, x_padded[..., 2:], x_padded[..., :-2]) * x_keep
    stacked = jnp.stack([centre, slope_depth, slope_lateral, slope_x], 0).transpose(2, 3, 0, 1, 4)
    blocks = stacked.reshape(layers * lateral, 8, width_x).astype(jnp.bfloat16)
    block_count = layers * lateral
    slot_count = recv_block.shape[1]
    source = jnp.arange(slot_count, dtype=jnp.int32) // CAP
    gathered = lax.all_gather(blocks, "tile", axis=0, tiled=True)
    fetched = gathered[source * block_count + recv_block[0]]
    alive_mask = (jnp.arange(slot_count, dtype=jnp.int32) % CAP < recv_count[0][source]).astype(
        jnp.float32
    )
    contribution = jnp.einsum(
        "jcno,jcfo->jfn",
        moments[0],
        fetched.reshape(slot_count, 4, 2, width_x),
        preferred_element_type=jnp.float32,
    )
    contribution = contribution * alive_mask[:, None, None]
    new_count = new_volume.shape[1]
    one_hot = (new_block[0][None, :] == jnp.arange(new_count, dtype=jnp.int32)[:, None]).astype(
        jnp.float32
    )
    summed = jnp.dot(
        one_hot, contribution.reshape(slot_count, 2 * width_x), precision=lax.Precision.HIGHEST
    )
    result = summed.reshape(new_count, 2, width_x) / new_volume[0][:, None, :]
    return result[None]


def solution(mesh):
    placed = (
        P(None, "depth", "tile", None),
        P("depth", "tile"),
        P("depth", "tile"),
        P("depth", "tile"),
        P("depth", "tile", None, None, None),
        P("depth", "tile", None),
    )
    return jax.shard_map(
        per_device,
        mesh=mesh,
        in_specs=placed,
        out_specs=P("depth", "tile", None, None),
        check_vma=False,
    )
```

profile of v0, /device:TPU:0, one launch (start us, length us, event | category | flops | bytes accessed | tf_op | source)
XLA Modules:
  0.0 171.6 jit_solution(12616896355087981375)
XLA Ops:
  6.5 0.0 copy-start
  6.5 0.0 all-gather.2.cloned.1.call-start
  6.5 1.0 fusion.26
  7.6 2.4 %collective-permute-start.1 = (f32[2,1,64,128]{3,2,1,0:T(8,128)S(1)}, f32[2,1,64,128]{3,2,1,0:T(8,128)S(1)}, u32[]{:S(2)}, u32[]{:S(2)}) collective-permute-start(f32[2,1,64,128]{3,2,1,0:T(8,128)S(1)} %get-tuple-element.12), channel_id=1, source_target_pairs={{0,8},{8,16},{16,24},{1,9},{9,17},{17,25},{2,10},{10,18},{18,26},{... | collective-permute-start | bytes 196616 | tf_op jit(solution)/shard_map/ppermute | solution.py:16
  9.9 1.3 collective-permute-start
  11.3 0.0 collective-permute-done.1
  11.3 3.9 %collective-permute-done = f32[2,1,64,128]{3,2,1,0:T(8,128)S(1)} collective-permute-done((f32[2,1,64,128]{3,2,1,0:T(8,128)S(1)}, f32[2,1,64,128]{3,2,1,0:T(8,128)S(1)}, u32[]{:S(2)}, u32[]{:S(2)}) %collective-permute-start) | collective-permute-done | bytes 65568 | tf_op jit(solution)/shard_map/ppermute | solution.py:17
  15.2 4.1 %convert_bitcast_fusion = (bf16[1,2,8,64,128]{4,3,2,1,0:T(8,128)(2,1)S(1)}, f32[2,10,64,128]{3,2,1,0:T(8,128)S(1)}, bf16[1,2,8,64,128]{4,3,2,1,0:T(8,128)(2,1)S(1)}, bf16[1,2,8,64,128]{4,3,2,1,0:T(8,128)(2,1)S(1)}) fusion(f32[2,8,64,128]{3,2,1,0:T(8,128)} %param.6, f32[2,10,64,128]{3,2,1,0:T(8,128)S(1)} %constant_dynamic-update-slice_fusion.2, ...), kind=kLoop, calls=%fused_computation.24 | loop fusion | flops 6684672 | bytes 1967104 | tf_op jit(solution)/shard_map/stack | solution.py:61
  19.3 1.3 collective-permute-start.2
  20.6 4.5 %collective-permute-start.3 = (f32[2,10,1,128]{3,2,1,0:T(1,128)S(1)}, f32[2,10,1,128]{3,2,1,0:T(1,128)S(1)}, u32[]{:S(2)}, u32[]{:S(2)}) collective-permute-start(f32[2,10,1,128]{3,2,1,0:T(1,128)S(1)} %get-tuple-element.6), channel_id=1, source_target_pairs={{0,1},{1,2},{2,3},{3,4},{4,5},{5,6},{6,7},{8,9},{9,10},{10,11},{11... | collective-permute-start | bytes 30728 | tf_op jit(solution)/shard_map/ppermute | solution.py:16
  25.2 0.0 collective-permute-done.2
  25.2 1.3 collective-permute-done.3
  26.6 0.9 fusion.16
  27.5 0.1 maximum_bitcast_fusion
  27.6 0.0 copy-start.1
  27.6 0.0 copy-start.4
  27.6 2.1 %copy.12 = bf16[8,64,4,2,128]{4,3,2,1,0:T(2,128)(2,1)} copy(bf16[8,64,4,2,128]{4,1,0,3,2:T(8,128)(2,1)S(1)} %maximum_bitcast_fusion) | data formatting | bytes 2097152 | tf_op jit(solution)/shard_map/convert_element_type | solution.py:62
  29.8 0.0 all-gather.2.cloned.1.call-update
  29.8 0.7 gather_fusion.1
  30.5 128.5 %all-gather.2.cloned.1.call-done = bf16[4096,8,128]{2,1,0:T(8,128)(2,1)} async-done(((bf16[512,8,128]{2,1,0:T(8,128)(2,1)}), bf16[4096,8,128]{2,1,0:T(8,128)(2,1)}) %all-gather.2.cloned.1.call-update) | async-done | bytes 8388624 | tf_op jit(solution)/shard_map/all_gather | solution.py:66
  159.0 4.0 %gather_fusion = bf16[16,8,128]{2,1,0:T(8,128)(2,1)S(1)} fusion(bf16[4096,8,128]{2,1,0:T(8,128)(2,1)} %all-gather.2.cloned.1.call-done, s32[1024]{0:T(1024)S(1)} %pad_clamp_fusion.1), kind=kCustom, calls=%fused_computation | custom fusion | bytes 65600 | tf_op jit(solution)/shard_map/gather | solution.py:67
  163.0 0.7 fusion.6
  163.7 0.3 fusion.2
  164.0 0.8 copy.14
  (20 shorter events, 0.1 us)
Async XLA Ops:
  6.5 156.5 %copy-start = (bf16[1,16,4,128,128]{4,3,2,1,0:T(8,128)(2,1)S(1)}, bf16[1,16,4,128,128]{4,3,2,1,0:T(8,128)(2,1)}, u32[]{:S(2)}) copy-start(bf16[1,16,4,128,128]{4,3,2,1,0:T(8,128)(2,1)} %param.10) | copy-start | bytes 6291460
  6.5 20.0 %copy-start.2 = (f32[2,8,64,128]{3,2,1,0:T(8,128)S(1)}, f32[2,8,64,128]{3,2,1,0:T(8,128)}, u32[]{:S(2)}) copy-start(f32[2,8,64,128]{3,2,1,0:T(8,128)} %param.6) | copy-start | bytes 1572868
  6.5 152.5 %all-gather.2.cloned.1.call-start = ((), (), s32[]{:S(2)}) async-start(), calls=%async_computation | async-start | bytes 9437184 | tf_op jit(solution)/shard_map/all_gather | solution.py:66
  7.6 3.7 %collective-permute-start.1 = (f32[2,1,64,128]{3,2,1,0:T(8,128)S(1)}, f32[2,1,64,128]{3,2,1,0:T(8,128)S(1)}, u32[]{:S(2)}, u32[]{:S(2)}) collective-permute-start(f32[2,1,64,128]{3,2,1,0:T(8,128)S(1)} %get-tuple-element.12), channel_id=1, source_target_pairs={{0,8},{8,16},{16,24},{1,9},{9,17},{17,25},{2,10},{10,18},{18,26},{... | collective-permute-start | bytes 196616 | tf_op jit(solution)/shard_map/ppermute | solution.py:16
  9.9 5.3 %collective-permute-start = (f32[2,1,64,128]{3,2,1,0:T(8,128)S(1)}, f32[2,1,64,128]{3,2,1,0:T(8,128)S(1)}, u32[]{:S(2)}, u32[]{:S(2)}) collective-permute-start(f32[2,1,64,128]{3,2,1,0:T(8,128)S(1)} %get-tuple-element.11), channel_id=1, source_target_pairs={{8,0},{16,8},{24,16},{9,1},{17,9},{25,17},{10,2},{18,10},{26,18},{... | collective-permute-start | bytes 196616 | tf_op jit(solution)/shard_map/ppermute | solution.py:17
  19.3 5.9 %collective-permute-start.2 = (f32[2,10,1,128]{3,2,1,0:T(1,128)S(1)}, f32[2,10,1,128]{3,2,1,0:T(1,128)S(1)}, u32[]{:S(2)}, u32[]{:S(2)}) collective-permute-start(f32[2,10,1,128]{3,2,1,0:T(1,128)S(1)} %get-tuple-element.5), channel_id=1, source_target_pairs={{1,0},{2,1},{3,2},{4,3},{5,4},{6,5},{7,6},{9,8},{10,9},{11,10},{12... | collective-permute-start | bytes 30728 | tf_op jit(solution)/shard_map/ppermute | solution.py:17
  20.6 5.9 %collective-permute-start.3 = (f32[2,10,1,128]{3,2,1,0:T(1,128)S(1)}, f32[2,10,1,128]{3,2,1,0:T(1,128)S(1)}, u32[]{:S(2)}, u32[]{:S(2)}) collective-permute-start(f32[2,10,1,128]{3,2,1,0:T(1,128)S(1)} %get-tuple-element.6), channel_id=1, source_target_pairs={{0,1},{1,2},{2,3},{3,4},{4,5},{5,6},{6,7},{8,9},{9,10},{10,11},{11... | collective-permute-start | bytes 30728 | tf_op jit(solution)/shard_map/ppermute | solution.py:16
  27.6 2.2 %copy-start.1 = (s32[1,8]{1,0:T(1,128)S(1)}, s32[1,8]{1,0:T(1,128)}, u32[]{:S(2)}) copy-start(s32[1,8]{1,0:T(1,128)} %param.8) | copy-start | bytes 100
  27.6 2.9 %copy-start.4 = (s32[1,16]{1,0:T(1,128)S(1)}, s32[1,16]{1,0:T(1,128)}, u32[]{:S(2)}) copy-start(s32[1,16]{1,0:T(1,128)} %param.7) | copy-start | bytes 196
  29.8 133.9 %copy-start.3 = (f32[1,128,128]{2,1,0:T(8,128)S(1)}, f32[1,128,128]{2,1,0:T(8,128)}, u32[]{:S(2)}) copy-start(f32[1,128,128]{2,1,0:T(8,128)} %param.11) | copy-start | bytes 196612
  29.8 133.9 %copy-start.5 = (s32[1,16]{1,0:T(1,128)S(1)}, s32[1,16]{1,0:T(1,128)}, u32[]{:S(2)}) copy-start(s32[1,16]{1,0:T(1,128)} %param.9) | copy-start | bytes 196
Sparse Core Ops, SparseCore 0:
  29.9 129.0 all-gather.1
where the time goes:
time: 172 us
  waiting for transfers between devices  134 us (78%)
  between operations  13.6 us (8%)
  starting transfers between devices  9.49 us (6%)
  local copies, waits for them, and re-layouts  8.61 us (5%)
  other arithmetic  5.17 us (3%)
    all_gather x1, waiting for transfers between devices, per_device(): gathered = lax.all_gather(blocks, 'tile', axis=0, tiled=True)  128 us
    ppermute x2, starting transfers between devices, with_halo(): before = lax.ppermute(last, axis, up)  6.91 us
    another operation x2, other arithmetic, per_device(): jnp.stack([centre, slope_depth, slope_lateral, slope_x], 0)  4.98 us
    gather x1, local copies, waits for them, and re-layouts, per_device(): fetched = gathered[source * block_count + recv_block[0]]  3.96 us
    ppermute x2, waiting for transfers between devices, with_halo(): after = lax.ppermute(initial, axis, down)  3.9 us
  transfers between devices with their start and end apart: 5, of which 3 were waited for; matrix products, arithmetic and copies ran while one was open for 0% of the time, Pallas kernels for 0%

commit v1 on v0

--- a/solution.py
+++ b/solution.py
@@ -1,9 +1,28 @@
+import functools
 import jax
 import jax.numpy as jnp
 from jax import lax
 from jax.sharding import PartitionSpec as P
+from jax.lax import axis_index, axis_size, ppermute
 
 CAP = 2
+
+
+def knots_get(local_block, dev_axis, at_axis):
+    total_devices = axis_size(dev_axis)
+    current_arr = sorted(((dev, (dev + 1) % total_devices) for dev in range(total_devices)))
+    mid_arr = local_block
+    history = [mid_arr]
+    for k0 in range(1, total_devices):
+        mid_arr = ppermute(mid_arr, axis_name=dev_axis, perm=current_arr)
+        history.insert(0, mid_arr)
+    near = jnp.concatenate(history, axis=at_axis)
+    w1 = axis_index(dev_axis)
+    everything = w1 + 1
+    return jnp.roll(near, everything * local_block.shape[at_axis], axis=at_axis)
+
+
+wrap_the_vectors = functools.partial(knots_get, dev_axis="tile", at_axis=0)
 
 
 def with_halo(array, sides, width):
@@ -63,7 +82,7 @@
     block_count = layers * lateral
     slot_count = recv_block.shape[1]
     source = jnp.arange(slot_count, dtype=jnp.int32) // CAP
-    gathered = lax.all_gather(blocks, "tile", axis=0, tiled=True)
+    gathered = wrap_the_vectors(blocks)
     fetched = gathered[source * block_count + recv_block[0]]
     alive_mask = (jnp.arange(slot_count, dtype=jnp.int32) % CAP < recv_count[0][source]).astype(
         jnp.float32

time: 172 us -> 238 us (1.38)
  waiting for transfers between devices: 134 us -> 187 us
  local copies, waits for them, and re-layouts: 8.61 us -> 29.9 us
  between operations: 13.6 us -> 0.34 us
  starting transfers between devices: 9.49 us -> 12.1 us
    ppermute x0 -> x7, waiting for transfers between devices: none -> 182 us  [knots_get(): mid_arr = ppermute(mid_arr, axis_name=dev_axis, perm=current_arr)]
    all_gather x1 -> x0, waiting for transfers between devices: 128 us -> none  [per_device(): gathered = lax.all_gather(blocks, 'tile', axis=0, tiled=True)]
    unnamed x13 -> x42, local copies, waits for them, and re-layouts: 0.03 us -> 18 us
    dynamic_slice x0 -> x1, local copies, waits for them, and re-layouts: none -> 3.65 us  [knots_get(): return jnp.roll(near, everything * local_block.shape[at_axis], axis=at_axis)]
    ppermute x0 -> x7, starting transfers between devices: none -> 2.62 us  [knots_get(): mid_arr = ppermute(mid_arr, axis_name=dev_axis, perm=current_arr)]
  transfers between devices with their start and end apart: 5 -> 11, of which waited for: 3 -> 9; matrix products, arithmetic and copies ran while one was open for 0% -> 1% of each run, Pallas kernels for 0% -> 0%
where the time goes in v1:
time: 238 us; the launch traced here: 237 us
  waiting for transfers between devices  187 us (79%)
  local copies, waits for them, and re-layouts  29.9 us (13%)
  starting transfers between devices  12.1 us (5%)
  other arithmetic  6.72 us (3%)
    ppermute x7, waiting for transfers between devices, knots_get(): mid_arr = ppermute(mid_arr, axis_name=dev_axis, perm=current_arr)  182 us
    unnamed x42, local copies, waits for them, and re-layouts  18 us
    ppermute x2, starting transfers between devices, with_halo(): before = lax.ppermute(last, axis, up)  6.91 us
    another operation x2, other arithmetic, per_device(): jnp.stack([centre, slope_depth, slope_lateral, slope_x], 0)  5.88 us
  transfers between devices with their start and end apart: 11, of which 9 were waited for; matrix products, arithmetic and copies ran while one was open for 1% of the time, Pallas kernels for 0%

profile of v1, /device:TPU:0, one launch (start us, length us, event | category | flops | bytes accessed | tf_op | source)
XLA Modules:
  0.0 237.1 jit_solution(9773187749108028282)
XLA Ops:
  1.0 2.4 collective-permute-start.1
  4.8 3.9 %collective-permute-done = f32[2,1,64,128]{3,2,1,0:T(8,128)S(1)} collective-permute-done((f32[2,1,64,128]{3,2,1,0:T(8,128)S(1)}, f32[2,1,64,128]{3,2,1,0:T(8,128)S(1)}, u32[]{:S(2)}, u32[]{:S(2)}) %collective-permute-start) | collective-permute-done | bytes 65568 | tf_op jit(solution)/shard_map/ppermute | solution.py:36
  8.7 3.9 %convert_bitcast_fusion = (bf16[1,2,8,64,128]{4,3,2,1,0:T(8,128)(2,1)S(1)}, f32[2,10,64,128]{3,2,1,0:T(8,128)S(1)}, bf16[1,2,8,64,128]{4,3,2,1,0:T(8,128)(2,1)S(1)}, bf16[1,2,8,64,128]{4,3,2,1,0:T(8,128)(2,1)S(1)}) fusion(f32[2,8,64,128]{3,2,1,0:T(8,128)} %param.6, f32[2,10,64,128]{3,2,1,0:T(8,128)S(1)} %constant_dynamic-update-slice_fusion.2, ...), kind=kLoop, calls=%fused_computation.24 | loop fusion | flops 6684672 | bytes 1967104 | tf_op jit(solution)/shard_map/stack | solution.py:80
  13.9 4.5 %collective-permute-start.3 = (f32[2,10,1,128]{3,2,1,0:T(1,128)S(1)}, f32[2,10,1,128]{3,2,1,0:T(1,128)S(1)}, u32[]{:S(2)}, u32[]{:S(2)}) collective-permute-start(f32[2,10,1,128]{3,2,1,0:T(1,128)S(1)} %get-tuple-element.6), channel_id=1, source_target_pairs={{0,1},{1,2},{2,3},{3,4},{4,5},{5,6},{6,7},{8,9},{9,10},{10,11},{11... | collective-permute-start | bytes 30728 | tf_op jit(solution)/shard_map/ppermute | solution.py:35
  18.5 1.3 collective-permute-done.3
  19.9 1.9 fusion.16
  23.0 2.5 %collective-permute-start.4 = (bf16[512,8,128]{2,1,0:T(8,128)(2,1)S(1)}, bf16[512,8,128]{2,1,0:T(8,128)(2,1)S(1)}, u32[]{:S(2)}, u32[]{:S(2)}) collective-permute-start(bf16[512,8,128]{2,1,0:T(8,128)(2,1)S(1)} %bitcast.55), channel_id=1, source_target_pairs={{0,1},{1,2},{2,3},{3,4},{4,5},{5,6},{6,7},{7,0},{8,9},{9,10},{10,1... | collective-permute-start | bytes 3145736 | tf_op jit(solution)/shard_map/ppermute | solution.py:17
  25.5 26.1 %collective-permute-done.4 = bf16[512,8,128]{2,1,0:T(8,128)(2,1)S(1)} collective-permute-done((bf16[512,8,128]{2,1,0:T(8,128)(2,1)S(1)}, bf16[512,8,128]{2,1,0:T(8,128)(2,1)S(1)}, u32[]{:S(2)}, u32[]{:S(2)}) %collective-permute-start.4) | collective-permute-done | bytes 1048608 | tf_op jit(solution)/shard_map/ppermute | solution.py:17
  52.8 28.2 %collective-permute-done.5 = bf16[512,8,128]{2,1,0:T(8,128)(2,1)S(1)} collective-permute-done((bf16[512,8,128]{2,1,0:T(8,128)(2,1)S(1)}, bf16[512,8,128]{2,1,0:T(8,128)(2,1)S(1)}, u32[]{:S(2)}, u32[]{:S(2)}) %collective-permute-start.5) | collective-permute-done | bytes 1048608 | tf_op jit(solution)/shard_map/ppermute | solution.py:17
  82.0 27.6 %collective-permute-done.6 = bf16[512,8,128]{2,1,0:T(8,128)(2,1)S(1)} collective-permute-done((bf16[512,8,128]{2,1,0:T(8,128)(2,1)S(1)}, bf16[512,8,128]{2,1,0:T(8,128)(2,1)S(1)}, u32[]{:S(2)}, u32[]{:S(2)}) %collective-permute-start.6) | collective-permute-done | bytes 1048608 | tf_op jit(solution)/shard_map/ppermute | solution.py:17
  110.6 26.7 %collective-permute-done.7 = bf16[512,8,128]{2,1,0:T(8,128)(2,1)S(1)} collective-permute-done((bf16[512,8,128]{2,1,0:T(8,128)(2,1)S(1)}, bf16[512,8,128]{2,1,0:T(8,128)(2,1)S(1)}, u32[]{:S(2)}, u32[]{:S(2)}) %collective-permute-start.7) | collective-permute-done | bytes 1048608 | tf_op jit(solution)/shard_map/ppermute | solution.py:17
  138.3 25.8 %collective-permute-done.8 = bf16[512,8,128]{2,1,0:T(8,128)(2,1)S(1)} collective-permute-done((bf16[512,8,128]{2,1,0:T(8,128)(2,1)S(1)}, bf16[512,8,128]{2,1,0:T(8,128)(2,1)S(1)}, u32[]{:S(2)}, u32[]{:S(2)}) %collective-permute-start.8) | collective-permute-done | bytes 1048608 | tf_op jit(solution)/shard_map/ppermute | solution.py:17
  165.1 25.0 %collective-permute-done.9 = bf16[512,8,128]{2,1,0:T(8,128)(2,1)} collective-permute-done((bf16[512,8,128]{2,1,0:T(8,128)(2,1)S(1)}, bf16[512,8,128]{2,1,0:T(8,128)(2,1)}, u32[]{:S(2)}, u32[]{:S(2)}) %collective-permute-start.9) | collective-permute-done | bytes 1048608 | tf_op jit(solution)/shard_map/ppermute | solution.py:17
  192.1 22.2 %collective-permute-done.10 = bf16[512,8,128]{2,1,0:T(8,128)(2,1)} collective-permute-done((bf16[512,8,128]{2,1,0:T(8,128)(2,1)}, bf16[512,8,128]{2,1,0:T(8,128)(2,1)}, u32[]{:S(2)}, u32[]{:S(2)}) %collective-permute-start.10) | collective-permute-done | bytes 1048608 | tf_op jit(solution)/shard_map/ppermute | solution.py:17
  215.7 1.4 constant_dynamic-update-slice_fusion.17
  217.0 1.4 constant_dynamic-update-slice_fusion.16
  218.4 1.4 constant_dynamic-update-slice_fusion.15
  219.8 1.4 constant_dynamic-update-slice_fusion.14
  221.1 1.4 constant_dynamic-update-slice_fusion.13
  222.5 1.4 constant_dynamic-update-slice_fusion.12
  224.0 1.4 constant_dynamic-update-slice_fusion.10
  225.4 1.4 constant_dynamic-update-slice_fusion.9
  227.7 3.6 %constant_dynamic-slice_fusion = bf16[4096,8,128]{2,1,0:T(8,128)(2,1)} fusion(bf16[8192,8,128]{2,1,0:T(8,128)(2,1)S(1)} %constant_dynamic-update-slice_fusion.3, s32[]{:T(128)S(6)} %select_n.62), kind=kLoop, calls=%fused_computation.69 | loop fusion | bytes 16777220 | tf_op jit(solution)/shard_map/jit(_roll_dynamic)/dynamic_slice | solution.py:22
  231.4 4.0 %gather_fusion = bf16[16,8,128]{2,1,0:T(8,128)(2,1)S(1)} fusion(bf16[4096,8,128]{2,1,0:T(8,128)(2,1)} %constant_dynamic-slice_fusion, s32[1024]{0:T(1024)S(1)} %get-tuple-element.14), kind=kCustom, calls=%fused_computation | custom fusion | bytes 65600 | tf_op jit(solution)/shard_map/gather | solution.py:86
  (61 shorter events, 16.0 us)
Async XLA Ops:
  0.0 235.3 %copy-start = (bf16[1,16,4,128,128]{4,3,2,1,0:T(8,128)(2,1)S(1)}, bf16[1,16,4,128,128]{4,3,2,1,0:T(8,128)(2,1)}, u32[]{:S(2)}) copy-start(bf16[1,16,4,128,128]{4,3,2,1,0:T(8,128)(2,1)} %param.10) | copy-start | bytes 6291460
  1.0 3.7 %collective-permute-start.1 = (f32[2,1,64,128]{3,2,1,0:T(8,128)S(1)}, f32[2,1,64,128]{3,2,1,0:T(8,128)S(1)}, u32[]{:S(2)}, u32[]{:S(2)}) collective-permute-start(f32[2,1,64,128]{3,2,1,0:T(8,128)S(1)} %get-tuple-element.12), channel_id=1, source_target_pairs={{0,8},{8,16},{16,24},{1,9},{9,17},{17,25},{2,10},{10,18},{18,26},{... | collective-permute-start | bytes 196616 | tf_op jit(solution)/shard_map/ppermute | solution.py:35
  3.4 5.3 %collective-permute-start = (f32[2,1,64,128]{3,2,1,0:T(8,128)S(1)}, f32[2,1,64,128]{3,2,1,0:T(8,128)S(1)}, u32[]{:S(2)}, u32[]{:S(2)}) collective-permute-start(f32[2,1,64,128]{3,2,1,0:T(8,128)S(1)} %get-tuple-element.11), channel_id=1, source_target_pairs={{8,0},{16,8},{24,16},{9,1},{17,9},{25,17},{10,2},{18,10},{26,18},{... | collective-permute-start | bytes 196616 | tf_op jit(solution)/shard_map/ppermute | solution.py:36
  12.6 5.9 %collective-permute-start.2 = (f32[2,10,1,128]{3,2,1,0:T(1,128)S(1)}, f32[2,10,1,128]{3,2,1,0:T(1,128)S(1)}, u32[]{:S(2)}, u32[]{:S(2)}) collective-permute-start(f32[2,10,1,128]{3,2,1,0:T(1,128)S(1)} %get-tuple-element.5), channel_id=1, source_target_pairs={{1,0},{2,1},{3,2},{4,3},{5,4},{6,5},{7,6},{9,8},{10,9},{11,10},{12... | collective-permute-start | bytes 30728 | tf_op jit(solution)/shard_map/ppermute | solution.py:36
  13.9 5.9 %collective-permute-start.3 = (f32[2,10,1,128]{3,2,1,0:T(1,128)S(1)}, f32[2,10,1,128]{3,2,1,0:T(1,128)S(1)}, u32[]{:S(2)}, u32[]{:S(2)}) collective-permute-start(f32[2,10,1,128]{3,2,1,0:T(1,128)S(1)} %get-tuple-element.6), channel_id=1, source_target_pairs={{0,1},{1,2},{2,3},{3,4},{4,5},{5,6},{6,7},{8,9},{9,10},{10,11},{11... | collective-permute-start | bytes 30728 | tf_op jit(solution)/shard_map/ppermute | solution.py:35
  23.0 28.6 %collective-permute-start.4 = (bf16[512,8,128]{2,1,0:T(8,128)(2,1)S(1)}, bf16[512,8,128]{2,1,0:T(8,128)(2,1)S(1)}, u32[]{:S(2)}, u32[]{:S(2)}) collective-permute-start(bf16[512,8,128]{2,1,0:T(8,128)(2,1)S(1)} %bitcast.55), channel_id=1, source_target_pairs={{0,1},{1,2},{2,3},{3,4},{4,5},{5,6},{6,7},{7,0},{8,9},{9,10},{10,1... | collective-permute-start | bytes 3145736 | tf_op jit(solution)/shard_map/ppermute | solution.py:17
  51.6 1.0 copy-start.1
  52.7 28.4 %collective-permute-start.5 = (bf16[512,8,128]{2,1,0:T(8,128)(2,1)S(1)}, bf16[512,8,128]{2,1,0:T(8,128)(2,1)S(1)}, u32[]{:S(2)}, u32[]{:S(2)}) collective-permute-start(bf16[512,8,128]{2,1,0:T(8,128)(2,1)S(1)} %collective-permute-done.4), channel_id=1, source_target_pairs={{0,1},{1,2},{2,3},{3,4},{4,5},{5,6},{6,7},{7,0},{8,9},{9,10},{10,1... | collective-permute-start | bytes 3145736 | tf_op jit(solution)/shard_map/ppermute | solution.py:17
  81.0 0.9 copy-start.3
  82.0 27.6 %collective-permute-start.6 = (bf16[512,8,128]{2,1,0:T(8,128)(2,1)S(1)}, bf16[512,8,128]{2,1,0:T(8,128)(2,1)S(1)}, u32[]{:S(2)}, u32[]{:S(2)}) collective-permute-start(bf16[512,8,128]{2,1,0:T(8,128)(2,1)S(1)} %collective-permute-done.5), channel_id=1, source_target_pairs={{0,1},{1,2},{2,3},{3,4},{4,5},{5,6},{6,7},{7,0},{8,9},{9,10},{10,1... | collective-permute-start | bytes 3145736 | tf_op jit(solution)/shard_map/ppermute | solution.py:17
  109.6 1.0 copy-start.5
  110.6 26.7 %collective-permute-start.7 = (bf16[512,8,128]{2,1,0:T(8,128)(2,1)S(1)}, bf16[512,8,128]{2,1,0:T(8,128)(2,1)S(1)}, u32[]{:S(2)}, u32[]{:S(2)}) collective-permute-start(bf16[512,8,128]{2,1,0:T(8,128)(2,1)S(1)} %collective-permute-done.6), channel_id=1, source_target_pairs={{0,1},{1,2},{2,3},{3,4},{4,5},{5,6},{6,7},{7,0},{8,9},{9,10},{10,1... | collective-permute-start | bytes 3145736 | tf_op jit(solution)/shard_map/ppermute | solution.py:17
  137.3 1.0 copy-start.7
  138.3 25.8 %collective-permute-start.8 = (bf16[512,8,128]{2,1,0:T(8,128)(2,1)S(1)}, bf16[512,8,128]{2,1,0:T(8,128)(2,1)S(1)}, u32[]{:S(2)}, u32[]{:S(2)}) collective-permute-start(bf16[512,8,128]{2,1,0:T(8,128)(2,1)S(1)} %collective-permute-done.7), channel_id=1, source_target_pairs={{0,1},{1,2},{2,3},{3,4},{4,5},{5,6},{6,7},{7,0},{8,9},{9,10},{10,1... | collective-permute-start | bytes 3145736 | tf_op jit(solution)/shard_map/ppermute | solution.py:17
  164.1 1.0 copy-start.9
  165.1 25.0 %collective-permute-start.9 = (bf16[512,8,128]{2,1,0:T(8,128)(2,1)S(1)}, bf16[512,8,128]{2,1,0:T(8,128)(2,1)}, u32[]{:S(2)}, u32[]{:S(2)}) collective-permute-start(bf16[512,8,128]{2,1,0:T(8,128)(2,1)S(1)} %collective-permute-done.8), channel_id=1, source_target_pairs={{0,1},{1,2},{2,3},{3,4},{4,5},{5,6},{6,7},{7,0},{8,9},{9,10},{10,1... | collective-permute-start | bytes 3145736 | tf_op jit(solution)/shard_map/ppermute | solution.py:17
  190.1 24.3 %collective-permute-start.10 = (bf16[512,8,128]{2,1,0:T(8,128)(2,1)}, bf16[512,8,128]{2,1,0:T(8,128)(2,1)}, u32[]{:S(2)}, u32[]{:S(2)}) collective-permute-start(bf16[512,8,128]{2,1,0:T(8,128)(2,1)} %collective-permute-done.9), channel_id=1, source_target_pairs={{0,1},{1,2},{2,3},{3,4},{4,5},{5,6},{6,7},{7,0},{8,9},{9,10},{10,1... | collective-permute-start | bytes 3145736 | tf_op jit(solution)/shard_map/ppermute | solution.py:17
  192.1 34.7 %copy-start.10 = (bf16[512,8,128]{2,1,0:T(8,128)(2,1)S(1)}, bf16[512,8,128]{2,1,0:T(8,128)(2,1)}, u32[]{:S(2)}) copy-start(bf16[512,8,128]{2,1,0:T(8,128)(2,1)} %copy-done.9) | copy-start | bytes 3145732
  192.1 34.8 %copy-start.8 = (bf16[512,8,128]{2,1,0:T(8,128)(2,1)S(1)}, bf16[512,8,128]{2,1,0:T(8,128)(2,1)}, u32[]{:S(2)}) copy-start(bf16[512,8,128]{2,1,0:T(8,128)(2,1)} %copy-done.7) | copy-start | bytes 3145732
  192.1 35.0 %copy-start.6 = (bf16[512,8,128]{2,1,0:T(8,128)(2,1)S(1)}, bf16[512,8,128]{2,1,0:T(8,128)(2,1)}, u32[]{:S(2)}) copy-start(bf16[512,8,128]{2,1,0:T(8,128)(2,1)} %copy-done.5) | copy-start | bytes 3145732
  192.1 35.1 %copy-start.4 = (bf16[512,8,128]{2,1,0:T(8,128)(2,1)S(1)}, bf16[512,8,128]{2,1,0:T(8,128)(2,1)}, u32[]{:S(2)}) copy-start(bf16[512,8,128]{2,1,0:T(8,128)(2,1)} %copy-done.3) | copy-start | bytes 3145732
  192.1 35.3 %copy-start.2 = (bf16[512,8,128]{2,1,0:T(8,128)(2,1)S(1)}, bf16[512,8,128]{2,1,0:T(8,128)(2,1)}, u32[]{:S(2)}) copy-start(bf16[512,8,128]{2,1,0:T(8,128)(2,1)} %copy-done.1) | copy-start | bytes 3145732
  225.4 10.6 %copy-start.11 = (f32[1,128,128]{2,1,0:T(8,128)S(1)}, f32[1,128,128]{2,1,0:T(8,128)}, u32[]{:S(2)}) copy-start(f32[1,128,128]{2,1,0:T(8,128)} %param.11) | copy-start | bytes 196612
  225.4 10.6 %copy-start.12 = (s32[1,16]{1,0:T(1,128)S(1)}, s32[1,16]{1,0:T(1,128)}, u32[]{:S(2)}) copy-start(s32[1,16]{1,0:T(1,128)} %param.9) | copy-start | bytes 196
